TPU v7x, 128 devices: a whole 4x4x4 slice. The times are simulated.
128 devices in a mesh: tile: 32 (over x, z, core), panel: 4 (over y).
Axes of the slice: x: 4, y: 4, z: 4, core: 2. Of those that a mesh axis runs over, the one named last changes fastest.
Arguments:
- masks: bfloat16 [512, 1024, 1024], P('tile', 'panel'), may hold values from -1 to 1
- cand_clip: int32 [2048], P('tile'), may hold values from 0 to 15
- cand_owner: int32 [2048], replicated, may hold values from 0 to 31, as said below
- cand_live: int32 [2048], replicated, may hold values from 0 to 1, as said below
- kernels: bfloat16 [32, 12, 64, 128], P('tile'), may hold values from -4 to 4
- weights: float32 [32, 12], P('tile'), may hold values from 0.05 to 0.5
- support_blocks: int32 [2], replicated, may hold values from 0 to 31, as said below
Outputs:
- intensity: bfloat16 [2048, 256, 256], P('tile', 'panel')
Inputs may be any that keep to these rules, and one draw needn't show every extreme that they name: `cand_owner`: each layout owner's 64 entries name every litho owner exactly 2 times. `cand_live`: some litho owner has all of its entries from every layout owner marked 1. `support_blocks`: distinct and ascending; the last is always block 31.
All inputs are finite; a program needn't handle non-finite values.
Results may differ from a plain program's by a relative error of at most 0.013.
Values may be sent and summed in bfloat16 or wider, within the bound.
No kernel may reach another device: no remote copies, remote signals or barrier semaphores. Data moves between devices by JAX's collectives and lax.ppermute only.
A program may use at most 192 MiB of HBM per device.

v0:
```python
import math

import jax
import jax.numpy as jnp
from jax import lax
from jax.sharding import PartitionSpec as P

BLK = 32
OUT = 256
SLOT = 2


def tables(positions, freqs, pixels, factor):
    phase = positions[:, None] * freqs[None, :] % pixels
    angle = phase.astype(jnp.float32) * (2.0 * math.pi / pixels)
    return (
        (jnp.cos(angle) * factor).astype(jnp.bfloat16),
        (jnp.sin(angle) * factor).astype(jnp.bfloat16),
    )


def picture_batch(spectra, kernel_sets, weight_sets, left_table, right_table):
    support = spectra.shape[1]
    width = right_table.shape[1] // 2
    s_re = spectra[:, None, :, :support]
    s_im = spectra[:, None, :, support:]
    k_re = kernel_sets[:, :, :, :support].astype(jnp.float32)
    k_im = kernel_sets[:, :, :, support:].astype(jnp.float32)
    field = jnp.concatenate([k_re * s_re - k_im * s_im, k_re * s_im + k_im * s_re], -1).astype(
        jnp.bfloat16
    )
    lowered = jnp.concatenate([-field[..., support:], field[..., :support]], -1)
    stacked = jnp.concatenate([field, lowered], 2)
    pupil_out = jnp.einsum(
        "ua,gkab->gkub", left_table, stacked, preferred_element_type=jnp.float32
    ).astype(jnp.bfloat16)
    groups, kernel_count, image_rows = (pupil_out.shape[0], pupil_out.shape[1], pupil_out.shape[2])
    amplitude = jnp.dot(
        pupil_out.reshape(-1, 2 * support), right_table, preferred_element_type=jnp.float32
    )
    amplitude = amplitude.reshape(groups, kernel_count, image_rows, 2 * width)
    power = amplitude[..., :width] ** 2 + amplitude[..., width:] ** 2
    return jnp.sum(weight_sets[:, :, None, None] * power, 1).astype(jnp.bfloat16)


def in_groups(spectra, kernel_sets, weight_sets, left_table, right_table):
    clip_count = spectra.shape[0]
    group_size = math.gcd(clip_count, 8)
    blocks = clip_count // group_size
    grouped = spectra.reshape((blocks, group_size) + spectra.shape[1:])

    def shared_step(spectrum_group):
        return picture_batch(spectrum_group, kernel_sets, weight_sets, left_table, right_table)

    images = lax.map(shared_step, grouped)
    return images.reshape((clip_count,) + images.shape[2:])


def partial_spectra(column_part, rows_cos, rows_sin):
    support = rows_cos.shape[1]
    swapped = jnp.concatenate([column_part[..., support:], -column_part[..., :support]], -1)
    row_left = jnp.concatenate([rows_cos, rows_sin], 0)
    return jnp.einsum(
        "rs,nrh->nsh",
        row_left,
        jnp.concatenate([column_part, swapped], 1),
        preferred_element_type=jnp.float32,
    )


def panel_total(partial_value):
    return lax.psum(partial_value.astype(jnp.bfloat16), "panel").astype(jnp.float32)


def shards(masks, cand_clip, cand_owner, cand_live, kernels, weights, support_blocks):
    owner_count = lax.axis_size("tile")
    tile_index = lax.axis_index("tile")
    panel_count = lax.axis_size("panel")
    panel_index = lax.axis_index("panel")
    held_count, mask_rows, pixels = masks.shape
    listed = cand_clip.shape[0]
    freqs = (support_blocks[:, None] * BLK + jnp.arange(BLK, dtype=jnp.int32)[None, :]).reshape(-1)
    support = freqs.shape[0]
    col_cos, col_sin = tables(jnp.arange(pixels, dtype=jnp.int32), freqs, pixels, pixels ** (-0.5))
    col_table = jnp.concatenate([col_cos, -col_sin], 1)
    own_rows = panel_index * mask_rows + jnp.arange(mask_rows, dtype=jnp.int32)
    rows_cos, rows_sin = tables(own_rows, freqs, pixels, pixels ** (-0.5))
    image_rows = OUT // panel_count
    stride = pixels // OUT
    full_cos, full_sin = tables(
        jnp.arange(OUT, dtype=jnp.int32) * stride, freqs, pixels, support ** (-0.5)
    )
    own_image = (panel_index * image_rows + jnp.arange(image_rows, dtype=jnp.int32)) * stride
    part_cos, part_sin = tables(own_image, freqs, pixels, support ** (-0.5))
    left_table = jnp.concatenate([part_cos, part_sin], 1)
    upper = jnp.concatenate([full_cos.T, full_sin.T], 1)
    lower = jnp.concatenate([-full_sin.T, full_cos.T], 1)
    right_table = jnp.concatenate([upper, lower], 0)
    own_owner = lax.dynamic_slice_in_dim(cand_owner, tile_index * listed, listed)
    own_live = lax.dynamic_slice_in_dim(cand_live, tile_index * listed, listed)
    targets = jnp.arange(owner_count, dtype=jnp.int32)
    onehot = (own_owner[None, :] == targets[:, None]).astype(jnp.int32)
    ranking = jnp.cumsum(onehot, 1) - 1
    slot_ids = jnp.arange(SLOT, dtype=jnp.int32)
    slot_match = onehot[:, None, :] * (ranking[:, None, :] == slot_ids[None, :, None]).astype(
        jnp.int32
    )
    send_index = jnp.sum(slot_match * jnp.arange(listed, dtype=jnp.int32)[None, None, :], 2)
    flat_index = send_index.reshape(-1)
    home_slot = (
        jnp.zeros((listed,), jnp.int32)
        .at[flat_index]
        .set(jnp.arange(owner_count * SLOT, dtype=jnp.int32))
    )
    sent_live = own_live[flat_index]
    sent_clip = cand_clip[flat_index]
    payload = jnp.take(masks, sent_clip, axis=0) * sent_live[:, None, None].astype(jnp.bfloat16)
    payload = payload.reshape(owner_count, SLOT, mask_rows, pixels)
    received = lax.all_to_all(payload, "tile", split_axis=0, concat_axis=0, tiled=True)
    clip_count = received.shape[0] * received.shape[1]
    flattened = received.reshape(clip_count * mask_rows, pixels)
    column_part = jnp.dot(flattened, col_table, preferred_element_type=jnp.float32).astype(
        jnp.bfloat16
    )
    image_column_part = column_part.reshape(clip_count, mask_rows, 2 * support)
    totals = panel_total(partial_spectra(image_column_part, rows_cos, rows_sin))
    images = in_groups(totals, kernels, weights, left_table, right_table)
    pictures = images.reshape(received.shape[0], received.shape[1], image_rows, OUT)
    returned = lax.all_to_all(pictures, "tile", split_axis=0, concat_axis=0, tiled=True)
    result = jnp.take(returned.reshape(owner_count * SLOT, image_rows, OUT), home_slot, axis=0)
    return result


def solution(mesh):
    return jax.shard_map(
        shards,
        mesh=mesh,
        in_specs=(
            P("tile", "panel", None),
            P("tile"),
            P(),
            P(),
            P("tile", None, None, None),
            P("tile", None),
            P(),
        ),
        out_specs=P("tile", "panel", None),
        check_vma=False,
    )
```

profile of v0, /device:TPU:1, one launch (start us, length us, event | category | flops | bytes accessed | tf_op | source)
XLA Modules:
  0.0 867.4 jit_solution(15704897088363990628)
XLA Ops:
  6.5 0.8 dynamic_slice.10
  7.9 1.4 gather_fusion
  9.5 0.8 gather_fusion.2
  10.5 15.9 %gather_fusion.1 = bf16[64,256,1024]{2,1,0:T(8,128)(2,1)} fusion(bf16[16,256,1024]{2,1,0:T(8,128)(2,1)} %param.9, s32[1024]{0:T(1024)S(1)} %pad_clamp_fusion.1), kind=kCustom, calls=%fused_computation.1 | custom fusion | bytes 67109120 | tf_op jit(solution)/shard_map/jit(_take)/gather | solution.py:117
  26.4 22.8 %select_multiply_fusion = bf16[32,2,256,1024]{3,2,1,0:T(8,128)(2,1)} fusion(bf16[32,2,256,1024]{3,2,1,0:T(8,128)(2,1)} %bitcast.57, pred[32,2]{1,0:T(8,128)(4,1)S(1)} %compare_and_fusion, bf16[32,2]{1,0:T(8,128)(2,1)S(1)} %convert_element_type.97), kind=kLoop, calls=%fused_computation.31 | loop fusion | flops 33554432 | bytes 67109056 | tf_op jit(solution)/shard_map/mul | solution.py:117
  49.2 9.6 %all-to-all-start = ((bf16[32,2,256,1024]{3,2,1,0:T(8,128)(2,1)}), bf16[32,2,256,1024]{3,2,1,0:T(8,128)(2,1)}, u32[]{:S(2)}, u32[]{:S(2)}) async-start(bf16[32,2,256,1024]{3,2,1,0:T(8,128)(2,1)} %select_multiply_fusion), calls=%async_computation | async-start | bytes 67108864 | tf_op jit(solution)/shard_map/all_to_all | solution.py:119
  59.4 1.0 fusion.44
  60.4 1.0 multiply_convert_fusion.1
  61.5 491.4 %all-to-all-done = bf16[32,2,256,1024]{3,2,1,0:T(8,128)(2,1)} async-done(((bf16[32,2,256,1024]{3,2,1,0:T(8,128)(2,1)}), bf16[32,2,256,1024]{3,2,1,0:T(8,128)(2,1)}, u32[]{:S(2)}, u32[]{:S(2)}) %all-to-all-start) | async-done | bytes 33554464 | tf_op jit(solution)/shard_map/all_to_all | solution.py:119
  552.9 15.1 %convolution_convert_fusion = bf16[16384,128]{1,0:T(8,128)(2,1)S(1)} fusion(bf16[16384,1024]{1,0:T(8,128)(2,1)} %bitcast.14, bf16[1024,64]{0,1:T(8,128)(2,1)S(1)} %fusion.44, bf16[1024,64]{0,1:T(8,128)(2,1)S(1)} %multiply_convert_fusion.1), kind=kOutput, calls=%fused_computation.32 | convolution fusion | flops 4297588736 | bytes 38010880 | tf_op jit(solution)/shard_map/dot_general | solution.py:122
  568.0 1.7 fusion.65
  569.7 4.7 fusion.32
  575.5 95.7 %all-reduce.2.cloned.1.call-done = bf16[8,8,64,128]{3,2,1,0:T(8,128)(2,1)} async-done(((bf16[8,8,64,128]{3,2,1,0:T(8,128)(2,1)}), bf16[8,8,64,128]{3,2,1,0:T(8,128)(2,1)}) %all-reduce.2.cloned.1.call-update) | async-done | bytes 1048592 | tf_op jit(solution)/shard_map/psum | solution.py:72
  671.2 1.5 reshape.166
  672.7 145.3 %while.10 = (s32[]{:T(128)}, bf16[8,8,64,256]{3,2,1,0:T(8,128)(2,1)}, f32[1,12]{1,0:T(1,128)S(1)}, bf16[1,12,64,128]{3,2,1,0:T(8,128)(2,1)S(1)}, f32[8,8,64,128]...) while((s32[]{:T(128)}, ...), condition=%wide.region_6.7_spmd, body=%wide.region_4.6_spmd.sunk | while | flops 1032945664 | bytes 50545344 | solution.py:55
  673.0 1.0 copy-done.3
  674.0 0.8 add_convert_fusion.2
  674.9 1.7 fusion.80
  676.6 7.8 fusion.81
  684.4 5.7 fusion.82
  690.2 0.7 bitcast_dynamic-update-slice_fusion.2
  691.2 1.0 copy-done.3
  692.2 0.8 add_convert_fusion.2
  693.0 1.7 fusion.80
  694.7 7.8 fusion.81
  702.6 5.7 fusion.82
  708.3 0.7 bitcast_dynamic-update-slice_fusion.2
  709.3 1.0 copy-done.3
  710.4 0.8 add_convert_fusion.2
  711.2 1.7 fusion.80
  712.9 7.8 fusion.81
  720.7 5.7 fusion.82
  727.5 1.0 copy-done.3
  728.5 0.8 add_convert_fusion.2
  729.4 1.7 fusion.80
  731.1 7.8 fusion.81
  738.9 5.7 fusion.82
  744.6 0.7 bitcast_dynamic-update-slice_fusion.2
  745.7 1.0 copy-done.3
  746.7 0.8 add_convert_fusion.2
  747.5 1.7 fusion.80
  749.2 7.8 fusion.81
  757.1 5.7 fusion.82
  763.8 1.0 copy-done.3
  764.9 0.8 add_convert_fusion.2
  765.7 1.7 fusion.80
  767.4 7.8 fusion.81
  775.2 5.7 fusion.82
  781.0 0.7 bitcast_dynamic-update-slice_fusion.2
  782.0 1.0 copy-done.3
  783.0 0.8 add_convert_fusion.2
  783.9 1.7 fusion.80
  785.6 7.8 fusion.81
  793.4 5.7 fusion.82
  800.2 1.0 copy-done.3
  801.2 0.8 add_convert_fusion.2
  802.0 1.7 fusion.80
  803.7 7.8 fusion.81
  811.6 5.7 fusion.82
  818.0 9.1 %all-to-all-start.1 = ((bf16[32,2,64,256]{3,2,1,0:T(8,128)(2,1)}), bf16[32,2,64,256]{3,2,1,0:T(8,128)(2,1)S(1)}, u32[]{:S(2)}, u32[]{:S(2)}) async-start(bf16[32,2,64,256]{3,2,1,0:T(8,128)(2,1)} %bitcast.19), calls=%async_computation.1 | async-start | bytes 4194304 | tf_op jit(solution)/shard_map/all_to_all | solution.py:129
  827.1 0.8 scatter_custom_fusion
  828.0 27.5 %all-to-all-done.1 = bf16[32,2,64,256]{3,2,1,0:T(8,128)(2,1)S(1)} async-done(((bf16[32,2,64,256]{3,2,1,0:T(8,128)(2,1)}), bf16[32,2,64,256]{3,2,1,0:T(8,128)(2,1)S(1)}, u32[]{:S(2)}, u32[]{:S(2)}) %all-to-all-start.1) | async-done | bytes 2097184 | tf_op jit(solution)/shard_map/all_to_all | solution.py:129
  855.4 2.0 gather_fusion.3
  857.4 3.2 broadcast_select_fusion
  (96 shorter events, 7.6 us)
Async XLA Ops:
  6.5 2.9 copy-start
  49.2 9.7 %copy-start.6 = (s32[2]{0:T(128)S(1)}, s32[2]{0:T(128)}, u32[]{:S(2)}) copy-start(s32[2]{0:T(128)} %param.15) | copy-start | bytes 28
  49.2 503.7 %all-to-all-start = ((bf16[32,2,256,1024]{3,2,1,0:T(8,128)(2,1)}), bf16[32,2,256,1024]{3,2,1,0:T(8,128)(2,1)}, u32[]{:S(2)}, u32[]{:S(2)}) async-start(bf16[32,2,256,1024]{3,2,1,0:T(8,128)(2,1)} %select_multiply_fusion), calls=%async_computation | async-start | bytes 67108864 | tf_op jit(solution)/shard_map/all_to_all | solution.py:119
  58.8 612.4 %all-reduce.2.cloned.1.call-start = ((), (), s32[]{:S(2)}) async-start(), calls=%async_computation.2 | async-start | bytes 2097152 | tf_op jit(solution)/shard_map/psum | solution.py:72
  574.4 98.2 %copy-start.2 = (bf16[1,12,64,128]{3,2,1,0:T(8,128)(2,1)S(1)}, bf16[1,12,64,128]{3,2,1,0:T(8,128)(2,1)}, u32[]{:S(2)}) copy-start(bf16[1,12,64,128]{3,2,1,0:T(8,128)(2,1)} %param.13) | copy-start | bytes 589828
  574.4 98.2 %copy-start.5 = (f32[1,12]{1,0:T(1,128)S(1)}, f32[1,12]{1,0:T(1,128)}, u32[]{:S(2)}) copy-start(f32[1,12]{1,0:T(1,128)} %param.14) | copy-start | bytes 148
  672.7 1.3 copy-start.3
  684.4 6.5 copy-start.4
  690.9 1.3 copy-start.3
  702.6 6.5 copy-start.4
  709.0 1.3 copy-start.3
  720.7 6.5 copy-start.4
  727.2 1.3 copy-start.3
  738.9 6.5 copy-start.4
  745.4 1.3 copy-start.3
  757.1 6.5 copy-start.4
  763.5 1.3 copy-start.3
  775.2 6.5 copy-start.4
  781.7 1.3 copy-start.3
  793.4 6.5 copy-start.4
  799.9 1.3 copy-start.3
  811.6 6.5 copy-start.4
  818.0 37.4 %all-to-all-start.1 = ((bf16[32,2,64,256]{3,2,1,0:T(8,128)(2,1)}), bf16[32,2,64,256]{3,2,1,0:T(8,128)(2,1)S(1)}, u32[]{:S(2)}, u32[]{:S(2)}) async-start(bf16[32,2,64,256]{3,2,1,0:T(8,128)(2,1)} %bitcast.19), calls=%async_computation.1 | async-start | bytes 4194304 | tf_op jit(solution)/shard_map/all_to_all | solution.py:129
  855.4 5.2 copy-start.1
Sparse Core Ops, SparseCore 0:
  574.6 96.5 all-reduce.1
where the time goes:
time: 868 us; the launch traced here: 867 us
  waiting for transfers between devices  615 us (71%)
  other arithmetic  100 us (12%)
  matrix products  82.4 us (9%)
  local copies, waits for them, and re-layouts  37.5 us (4%)
  starting transfers between devices  18.8 us (2%)
  between operations  13.6 us (2%)
    all_to_all x1, waiting for transfers between devices, shards(): lax.all_to_all(payload, 'tile', split_axis=0, concat_axis=0, tiled=True)  491 us
    psum x1, waiting for transfers between devices, panel_total(): lax.psum(partial_value.astype(jnp.bfloat16), 'panel').astype(jnp.float32)  95.7 us
    dot_general x8, matrix products, picture_batch(): jnp.dot(pupil_out.reshape(-1, 2 * support), right_table, preferred_elemen...  62.6 us
    reduce_sum x8, other arithmetic, picture_batch(): jnp.sum(weight_sets[:, :, None, None] * power, 1).astype(jnp.bfloat16)  45.9 us
    all_to_all x1, waiting for transfers between devices, shards(): lax.all_to_all(pictures, 'tile', split_axis=0, concat_axis=0, tiled=True)  27.5 us
    mul x1, other arithmetic, shards(): jnp.take(masks, sent_clip, axis=0)  22.8 us
  transfers between devices with their start and end apart: 3, of which 3 were waited for; matrix products, arithmetic and copies ran while one was open for 1% of the time, Pallas kernels for 0%

commit v1 on v0

v1 whole, which is shorter than its diff:
```python
import functools
import math

import jax
import jax.numpy as jnp
import numpy as np
from jax import lax
from jax.experimental import pallas as pl
from jax.experimental.pallas import tpu as pltpu
from jax.sharding import PartitionSpec as P

BLK = 32
OUT = 256
SIDE = 4
CORES = 2
OUT_SLOTS = 4
KERNEL_SLOTS = 3
GROUP = 16
F32 = jnp.float32
BF16 = jnp.bfloat16


def block_tables(pixels):
    phase = np.arange(pixels)[:, None] * np.arange(pixels)[None, :] % pixels
    angle = phase * (2.0 * math.pi / pixels)
    factor = pixels ** (-0.5)
    blocks = pixels // BLK
    cos = (np.cos(angle) * factor).reshape(pixels, blocks, BLK).transpose(1, 0, 2)
    sin = (np.sin(angle) * factor).reshape(pixels, blocks, BLK).transpose(1, 0, 2)
    gap = np.zeros_like(cos)
    return np.concatenate([cos, gap, -sin, gap], -1).astype(jnp.bfloat16)


def swap_halves(value):
    return pltpu.roll(value, value.shape[-1] // 2, value.ndim - 1)


def spectrum_body(
    place, masks, first, second, partial, left, right, whole, table, row_table
):
    pixels, lanes = table.shape
    mask_rows = masks.shape[1]
    image_rows = left.shape[0]
    half = lanes // 2
    stride = pixels // OUT

    @pl.when(pl.program_id(0) == 0)
    def _():
        whole[...] = first[0].astype(F32) + pltpu.roll(second[0].astype(F32), BLK, 1)
        table[...] = whole[...].astype(BF16)
        start = place[2] * mask_rows
        own = whole[pl.ds(pl.multiple_of(start, mask_rows), mask_rows), :]
        row_table[...] = own.T.astype(BF16)
        scale = math.sqrt(pixels / half)
        sign = jnp.where(lax.broadcasted_iota(jnp.int32, (image_rows, lanes), 1) < half, scale, -scale)
        own_image = whole[pl.ds(pl.multiple_of(start, mask_rows), image_rows, stride=stride), :]
        left[...] = (own_image * sign).astype(BF16)
        image = (whole[pl.ds(0, OUT, stride=stride), :] * scale).T
        right[:, :OUT] = image.astype(BF16)
        right[:half, OUT:] = (-image[half:]).astype(BF16)
        right[half:, OUT:] = image[:half].astype(BF16)

    count = masks.shape[0]
    columns = jnp.dot(
        masks[...].reshape(count * mask_rows, pixels), table[...], preferred_element_type=F32
    ).astype(BF16)
    sign = jnp.where(lax.broadcasted_iota(jnp.int32, (half, lanes), 1) < half, -1.0, 1.0)
    for clip in range(count):
        both = jnp.dot(
            row_table[...],
            columns[clip * mask_rows : (clip + 1) * mask_rows],
            preferred_element_type=F32,
        )
        partial[clip] = (both[:half] + swap_halves(both[half:]) * sign).astype(BF16)


def partial_spectra(masks, place, tables):
    held, mask_rows, pixels = masks.shape
    lanes = tables.shape[2]
    image_rows = mask_rows * OUT // pixels
    step = math.gcd(held, 2)
    return pl.pallas_call(
        spectrum_body,
        grid_spec=pltpu.PrefetchScalarGridSpec(
            num_scalar_prefetch=1,
            grid=(held // step,),
            in_specs=[
                pl.BlockSpec((step, mask_rows, pixels), lambda i, place: (i, 0, 0)),
                pl.BlockSpec((1, pixels, lanes), lambda i, place: (place[0], 0, 0)),
                pl.BlockSpec((1, pixels, lanes), lambda i, place: (place[1], 0, 0)),
            ],
            out_specs=[
                pl.BlockSpec((step, lanes // 2, lanes), lambda i, place: (i, 0, 0)),
                pl.BlockSpec((image_rows, lanes), lambda i, place: (0, 0)),
                pl.BlockSpec((lanes, 2 * OUT), lambda i, place: (0, 0)),
            ],
            scratch_shapes=[
                pltpu.VMEM((pixels, lanes), F32),
                pltpu.VMEM((pixels, lanes), BF16),
                pltpu.VMEM((lanes, mask_rows), BF16),
            ],
        ),
        out_shape=[
            jax.ShapeDtypeStruct((held, lanes // 2, lanes), BF16),
            jax.ShapeDtypeStruct((image_rows, lanes), BF16),
            jax.ShapeDtypeStruct((lanes, 2 * OUT), BF16),
        ],
        compiler_params=pltpu.CompilerParams(vmem_limit_bytes=32 << 20),
        cost_estimate=pl.CostEstimate(
            flops=2 * held * mask_rows * pixels * lanes,
            bytes_accessed=2 * held * mask_rows * pixels,
            transcendentals=0,
        ),
    )(place, masks, tables, tables)


def spread(spectrum):
    half = spectrum.shape[1] // 2
    low = lax.broadcasted_iota(jnp.int32, spectrum.shape, 1) < half
    other = swap_halves(spectrum)
    return (
        jnp.where(low, spectrum, other),
        jnp.where(low, -other, spectrum),
        jnp.where(low, -other, -spectrum),
        jnp.where(low, -spectrum, other),
    )


def first_product(kernel_set, factors, left, pupil):
    kernel_count = kernel_set.shape[0]
    rows = left.shape[0]
    lanes = kernel_set.shape[2]
    straight, crossed, lowered, lowered_crossed = factors
    columns = []
    for k in range(kernel_count):
        kernel = kernel_set[k].astype(F32)
        other = swap_halves(kernel)
        field = (kernel * straight + other * crossed).astype(BF16)
        below = (kernel * lowered + other * lowered_crossed).astype(BF16)
        columns.append(jnp.concatenate([field, below], 0))
    product = jnp.dot(left, jnp.concatenate(columns, 1), preferred_element_type=F32).astype(BF16)
    for k in range(kernel_count):
        pupil[k * rows : (k + 1) * rows, :] = product[:, k * lanes : (k + 1) * lanes]


def second_product(pupil, right, rows):
    amplitude = jnp.dot(pupil[...], right[...], preferred_element_type=F32)
    real, imag = amplitude[:, :OUT], amplitude[:, OUT:]
    power = real * real + imag * imag
    total = power[:rows]
    for k in range(1, power.shape[0] // rows):
        total = total + power[k * rows : (k + 1) * rows]
    return total.astype(BF16)


def imaging_body(group, sets, *refs):
    entries, near, far, left, right = refs[:5]
    sources = refs[5 : 5 + sets]
    images = refs[-9]
    held_kernels, even, odd, out_buffer, zeros, kernel_sems, out_sems, zero_sem = refs[-8:]
    base = group * GROUP
    rows = left.shape[0]
    per_set = sources[0].shape[0]

    live = lax.fori_loop(0, GROUP, lambda i, n: n + (entries[base + i] >> 13), jnp.int32(0))

    def place(e):
        return entries[base + e] & 63

    def fetch(e):
        slot = (entries[base + e] >> 6) & 7
        buffer = lax.rem(e, KERNEL_SLOTS)
        for which in range(sets):

            @pl.when((slot >= which * per_set) & (slot < (which + 1) * per_set))
            def _():
                pltpu.make_async_copy(
                    sources[which].at[slot - which * per_set],
                    held_kernels.at[buffer],
                    kernel_sems.at[buffer],
                ).start()

    def fetched(e):
        buffer = lax.rem(e, KERNEL_SLOTS)
        pltpu.make_async_copy(
            sources[0].at[0], held_kernels.at[buffer], kernel_sems.at[buffer]
        ).wait()
        return held_kernels.at[buffer]

    def put(e):
        buffer = lax.rem(e, OUT_SLOTS)
        return pltpu.make_async_copy(
            out_buffer.at[buffer], images.at[place(e)], out_sems.at[buffer]
        )

    def put_zeros(e):
        return pltpu.make_async_copy(zeros, images.at[place(e)], zero_sem)

    def factors(e):
        clip = (entries[base + e] >> 9) & 15
        return spread(near[clip].astype(F32) + far[clip].astype(F32))

    @pl.when(live < GROUP)
    def _():
        zeros[...] = jnp.zeros_like(zeros)
        lax.fori_loop(live, GROUP, lambda e, _: put_zeros(e).start(), None)

    @pl.when(live > 0)
    def _():
        fetch(0)

        @pl.when(live > 1)
        def _():
            fetch(1)

        first_product(fetched(0), factors(0), left[...], even)

    pupils = (even, odd)

    def pair(i, _):
        for parity in (0, 1):
            e = 2 * i + parity

            @pl.when(e + 2 < live)
            def _():
                fetch(e + 2)

            @pl.when((e >= OUT_SLOTS) & (e < live))
            def _():
                put(e - OUT_SLOTS).wait()

            @pl.when(e + 1 < live)
            def _():
                fetched(e + 1)

            ahead = jnp.minimum(e + 1, GROUP - 1)
            picture = second_product(pupils[parity], right, rows)
            first_product(
                held_kernels.at[lax.rem(e + 1, KERNEL_SLOTS)],
                factors(ahead),
                left[...],
                pupils[1 - parity],
            )

            @pl.when(e < live)
            def _():
                out_buffer[lax.rem(e, OUT_SLOTS)] = picture
                put(e).start()

    lax.fori_loop(0, (live + 1) // 2, pair, None)
    for back in range(1, OUT_SLOTS + 1):

        @pl.when(live >= back)
        def _():
            put(live - back).wait()

    lax.fori_loop(live, GROUP, lambda e, _: put_zeros(e).wait(), None)


def imaging(group, entries, near, far, left, right, sources, images):
    rows = left.shape[0]
    kernel_count, support, lanes = sources[0].shape[1:]
    in_vmem = pl.BlockSpec(memory_space=pltpu.VMEM)
    anywhere = pl.BlockSpec(memory_space=pl.ANY)
    listed = entries.shape[0]
    operands = [entries, near, far, left, right, *sources]
    specs = [pl.BlockSpec(memory_space=pltpu.SMEM)] + [in_vmem] * 4 + [anywhere] * len(sources)
    aliases = {}
    if images is not None:
        aliases = {len(operands): 0}
        operands.append(images)
        specs.append(anywhere)
    return pl.pallas_call(
        functools.partial(imaging_body, group, len(sources)),
        in_specs=specs,
        out_specs=anywhere,
        out_shape=jax.ShapeDtypeStruct((listed, rows, OUT), BF16),
        input_output_aliases=aliases,
        scratch_shapes=[
            pltpu.VMEM((KERNEL_SLOTS, kernel_count, support, lanes), BF16),
            pltpu.VMEM((kernel_count * rows, lanes), BF16),
            pltpu.VMEM((kernel_count * rows, lanes), BF16),
            pltpu.VMEM((OUT_SLOTS, rows, OUT), BF16),
            pltpu.VMEM((rows, OUT), BF16),
            pltpu.SemaphoreType.DMA((KERNEL_SLOTS,)),
            pltpu.SemaphoreType.DMA((OUT_SLOTS,)),
            pltpu.SemaphoreType.DMA,
        ],
        compiler_params=pltpu.CompilerParams(vmem_limit_bytes=32 << 20),
        cost_estimate=pl.CostEstimate(
            flops=2 * GROUP * kernel_count * rows * lanes * (lanes + 2 * OUT),
            bytes_accessed=GROUP * kernel_count * support * lanes * 4,
            transcendentals=0,
        ),
    )(*operands)


def tile_of(x, z, core):
    return (x * SIDE + z) * CORES + core


def partners(axes, flip):
    pairs = []
    for x in range(SIDE):
        for z in range(SIDE):
            for core in range(CORES):
                there = (x ^ flip, z) if axes[core] == "x" else (x, z ^ flip)
                pairs.append((tile_of(x, z, core), tile_of(*there, core)))
    return pairs


def entry_list(cand_clip, own_owner, own_live, tile_index):
    listed = cand_clip.shape[0]
    core = tile_index & 1
    other_core = own_owner & 1
    across_x = (own_owner >> 3) ^ (tile_index >> 3)
    across_z = ((own_owner >> 1) ^ (tile_index >> 1)) & 3
    first = jnp.where(other_core == 0, across_x, across_z)
    second = jnp.where(other_core == 0, across_z, across_x)
    in_b = first >> 1
    mixed = (second >> 1) ^ (second & 1)
    high = second >> 1
    later = jnp.where(in_b == 1, mixed, high)
    pair = jnp.where(in_b == 1, high, mixed)
    slot = in_b * 4 + pair * 2 + ((first & 1) ^ in_b)
    call = later * 2 + (other_core ^ core)
    index = jnp.arange(listed, dtype=jnp.int32)
    key = ((call * 2 + 1 - own_live) * 8 + slot) * listed + index
    rank = jnp.sum((key[:, None] < key[None, :]).astype(jnp.int32), 0)
    packed = index + slot * 64 + cand_clip * 512 + own_live * 8192
    return jnp.sum(jnp.where(rank[:, None] == index[None, :], packed[:, None], 0), 0)


def shards(masks, cand_clip, cand_owner, cand_live, kernels, weights, support_blocks):
    tile_index = lax.axis_index("tile")
    panel_index = lax.axis_index("panel")
    listed = cand_clip.shape[0]
    send = lambda value, axes, flip: lax.ppermute(value, "tile", partners(axes, flip))
    across = lambda value: lax.ppermute(
        value, "tile", [(i, i ^ 1) for i in range(SIDE * SIDE * CORES)]
    )
    panel = lambda value, flip: lax.ppermute(value, "panel", [(i, i ^ flip) for i in range(SIDE)])

    scaled = kernels.astype(F32) * jnp.sqrt(weights)[:, :, None, None]
    own = scaled.astype(BF16)
    one = send(own, "xz", 1)
    three = send(own, "xz", 3)
    two = send(one, "xz", 3)

    tables = jnp.asarray(block_tables(masks.shape[2]))
    place = jnp.concatenate([support_blocks, panel_index[None].astype(jnp.int32)])
    partial, left, right = partial_spectra(masks, place, tables)
    near = (partial.astype(F32) + panel(partial, 1).astype(F32)).astype(BF16)
    far = panel(near, 3)

    own_owner = lax.dynamic_slice_in_dim(cand_owner, tile_index * listed, listed)
    own_live = lax.dynamic_slice_in_dim(cand_live, tile_index * listed, listed)
    entries = entry_list(cand_clip, own_owner, own_live, tile_index)

    half_a = jnp.concatenate([own, one], 0)
    half_b = jnp.concatenate([three, two], 0)
    four_a = jnp.concatenate([half_a, send(half_a, "zx", 1)], 0)
    four_b = jnp.concatenate([half_b, send(half_b, "zx", 3)], 0)
    later_a = send(four_a, "zx", 3)
    later_b = send(four_b, "zx", 1)
    sibling_a, sibling_b = across(four_a), across(four_b)
    last_a, last_b = across(later_a), across(later_b)

    images = None
    calls = [(four_a, four_b), (sibling_a, sibling_b), (later_a, later_b), (last_a, last_b)]
    for group, sources in enumerate(calls):
        images = imaging(group, entries, near, far, left, right, sources, images)
    return images


def solution(mesh):
    return jax.shard_map(
        shards,
        mesh=mesh,
        in_specs=(
            P("tile", "panel", None),
            P("tile"),
            P(),
            P(),
            P("tile", None, None, None),
            P("tile", None),
            P(),
        ),
        out_specs=P("tile", "panel", None),
        check_vma=False,
    )
```

time: 868 us -> 93.2 us (0.11)
  the two profiles are of different devices: /device:TPU:1 before, /device:TPU:88 now
where the time goes in v1:
time: 93.2 us; the launch traced here: 91.5 us
  Pallas kernels  44.2 us (47%)
  waiting for transfers between devices  22.1 us (24%)
  starting transfers between devices  13.6 us (15%)
  local copies, waits for them, and re-layouts  7.51 us (8%)
  other arithmetic  3.93 us (4%)
    pallas_call x4, Pallas kernels, imaging(): pl.pallas_call(functools.partial(imaging_body, group, len(sources)), in_s...  37.7 us
    ppermute x7, starting transfers between devices, shards(): lax.ppermute(value, 'tile', partners(axes, flip))  11.4 us
    ppermute x7, waiting for transfers between devices, shards(): lax.ppermute(value, 'tile', partners(axes, flip))  11.1 us
    ppermute x2, waiting for transfers between devices, shards(): lax.ppermute(value, 'panel', [(i, i ^ flip) for i in range(SIDE)])  11 us
    unnamed x6, local copies, waits for them, and re-layouts  6.8 us
    pallas_call x1, Pallas kernels, partial_spectra(): pl.pallas_call(spectrum_body, grid_spec=pltpu.PrefetchScalarGridSpec(num_...  6.53 us
  transfers between devices with their start and end apart: 13, of which 6 were waited for; matrix products, arithmetic and copies ran while one was open for 3% of the time, Pallas kernels for 40%

profile of v1, /device:TPU:88, one launch (start us, length us, event | category | flops | bytes accessed | tf_op | source)
XLA Modules:
  0.0 91.5 jit_solution(12689049889160255054)
XLA Ops:
  0.0 0.7 sqrt_bitcast_fusion
  0.7 1.0 %multiply_convert_fusion = bf16[1,12,64,128]{3,2,1,0:T(8,128)(2,1)S(1)} fusion(bf16[1,12,64,128]{3,2,1,0:T(8,128)(2,1)} %param.12, f32[12]{0:T(128)S(1)} %sqrt_bitcast_fusion), kind=kLoop, calls=%fused_computation.4 | loop fusion | flops 294912 | bytes 393264 | tf_op jit(solution)/shard_map/convert_element_type | solution.py:345
  1.7 1.6 %collective-permute-start.2 = (bf16[1,12,64,128]{3,2,1,0:T(8,128)(2,1)S(1)}, bf16[1,12,64,128]{3,2,1,0:T(8,128)(2,1)S(1)}, u32[]{:S(2)}, u32[]{:S(2)}) collective-permute-start(bf16[1,12,64,128]{3,2,1,0:T(8,128)(2,1)S(1)} %multiply_convert_fusion), channel_id=1, source_target_pairs={{0,32},{4,12},{8,40},{12,4},{16,48},{20,28},{24,56},{28,20},{32,0}... | collective-permute-start | bytes 589832 | tf_op jit(solution)/shard_map/ppermute | solution.py:338
  3.3 2.1 %collective-permute-start.6 = (bf16[1,12,64,128]{3,2,1,0:T(8,128)(2,1)S(1)}, bf16[1,12,64,128]{3,2,1,0:T(8,128)(2,1)S(1)}, u32[]{:S(2)}, u32[]{:S(2)}) collective-permute-start(bf16[1,12,64,128]{3,2,1,0:T(8,128)(2,1)S(1)} %multiply_convert_fusion), channel_id=1, source_target_pairs={{0,96},{4,28},{8,104},{12,20},{16,112},{20,12},{24,120},{28,4},{32... | collective-permute-start | bytes 589832 | tf_op jit(solution)/shard_map/ppermute | solution.py:338
  5.4 2.1 %collective-permute-done.2 = bf16[1,12,64,128]{3,2,1,0:T(8,128)(2,1)S(1)} collective-permute-done((bf16[1,12,64,128]{3,2,1,0:T(8,128)(2,1)S(1)}, bf16[1,12,64,128]{3,2,1,0:T(8,128)(2,1)S(1)}, u32[]{:S(2)}, u32[]{:S(2)}) %collective-permute-start.2) | collective-permute-done | bytes 196640 | tf_op jit(solution)/shard_map/ppermute | solution.py:338
  7.5 2.8 %collective-permute-start.7 = (bf16[1,12,64,128]{3,2,1,0:T(8,128)(2,1)S(1)}, bf16[1,12,64,128]{3,2,1,0:T(8,128)(2,1)S(1)}, u32[]{:S(2)}, u32[]{:S(2)}) collective-permute-start(bf16[1,12,64,128]{3,2,1,0:T(8,128)(2,1)S(1)} %collective-permute-done.2), channel_id=1, source_target_pairs={{0,96},{4,28},{8,104},{12,20},{16,112},{20,12},{24,120},{28,4},{32... | collective-permute-start | bytes 589832 | tf_op jit(solution)/shard_map/ppermute | solution.py:338
  10.2 1.7 %collective-permute-start.3 = (bf16[2,12,64,128]{3,2,1,0:T(8,128)(2,1)S(1)}, bf16[2,12,64,128]{3,2,1,0:T(8,128)(2,1)S(1)}, u32[]{:S(2)}, u32[]{:S(2)}) collective-permute-start(bf16[2,12,64,128]{3,2,1,0:T(8,128)(2,1)S(1)} %pad_maximum_fusion.1), channel_id=1, source_target_pairs={{0,8},{4,36},{8,0},{12,44},{16,24},{20,52},{24,16},{28,60},{32,40}... | collective-permute-start | bytes 1179656 | tf_op jit(solution)/shard_map/ppermute | solution.py:338
  12.0 0.0 collective-permute-done.6
  12.0 2.4 %collective-permute-done.7 = bf16[1,12,64,128]{3,2,1,0:T(8,128)(2,1)S(1)} collective-permute-done((bf16[1,12,64,128]{3,2,1,0:T(8,128)(2,1)S(1)}, bf16[1,12,64,128]{3,2,1,0:T(8,128)(2,1)S(1)}, u32[]{:S(2)}, u32[]{:S(2)}) %collective-permute-start.7) | collective-permute-done | bytes 196640 | tf_op jit(solution)/shard_map/ppermute | solution.py:338
  14.4 0.2 collective-permute-start.8
  14.6 0.7 pad_add_fusion.place
  15.3 2.8 %collective-permute-done.3 = bf16[2,12,64,128]{3,2,1,0:T(8,128)(2,1)S(1)} collective-permute-done((bf16[2,12,64,128]{3,2,1,0:T(8,128)(2,1)S(1)}, bf16[2,12,64,128]{3,2,1,0:T(8,128)(2,1)S(1)}, u32[]{:S(2)}, u32[]{:S(2)}) %collective-permute-start.3) | collective-permute-done | bytes 393248 | tf_op jit(solution)/shard_map/ppermute | solution.py:338
  18.1 0.1 pad_maximum_fusion.refs_5_
  18.2 0.2 collective-permute-start.4
  18.4 3.9 %collective-permute-done.8 = bf16[2,12,64,128]{3,2,1,0:T(8,128)(2,1)S(1)} collective-permute-done((bf16[2,12,64,128]{3,2,1,0:T(8,128)(2,1)S(1)}, bf16[2,12,64,128]{3,2,1,0:T(8,128)(2,1)S(1)}, u32[]{:S(2)}, u32[]{:S(2)}) %collective-permute-start.8) | collective-permute-done | bytes 393248 | tf_op jit(solution)/shard_map/ppermute | solution.py:338
  22.2 0.1 constant_dynamic-update-slice_fusion.refs_6_
  22.3 2.9 %collective-permute-start.9 = (bf16[4,12,64,128]{3,2,1,0:T(8,128)(2,1)S(1)}, bf16[4,12,64,128]{3,2,1,0:T(8,128)(2,1)S(1)}, u32[]{:S(2)}, u32[]{:S(2)}) collective-permute-start(bf16[4,12,64,128]{3,2,1,0:T(8,128)(2,1)S(1)} %constant_dynamic-update-slice_fusion.refs_6_), channel_id=1, source_target_pairs={{0,8},{4,36},{8,0},{12,44},{16,24},{20,52},{24,16},{28,60},{32,40}... | collective-permute-start | bytes 2359304 | tf_op jit(solution)/shard_map/ppermute | solution.py:338
  25.2 0.0 copy-start
  25.2 3.4 %copy-done = bf16[32,1024,128]{2,1,0:T(8,128)(2,1)S(1)} copy-done((bf16[32,1024,128]{2,1,0:T(8,128)(2,1)S(1)}, bf16[32,1024,128]{2,1,0:T(8,128)(2,1)}, u32[]{:S(2)}) %copy-start) | copy-done | bytes 8388632
  28.6 0.0 copy-start.1
  28.6 3.4 %copy-done.1 = bf16[16,256,1024]{2,1,0:T(8,128)(2,1)S(1)} copy-done((bf16[16,256,1024]{2,1,0:T(8,128)(2,1)S(1)}, bf16[16,256,1024]{2,1,0:T(8,128)(2,1)}, u32[]{:S(2)}) %copy-start.1) | copy-done | bytes 8388632
  32.0 6.5 %shard_map.82 = (bf16[16,64,128]{2,1,0:T(8,128)(2,1)S(1)}, bf16[64,128]{1,0:T(8,128)(2,1)S(1)}, bf16[128,512]{1,0:T(8,128)(2,1)S(1)}) custom-call(s32[3]{0:T(128)S(1)} %pad_add_fusion.place, bf16[16,256,1024]{2,1,0:T(8,128)(2,1)S(1)} %copy-done.1, bf16[32,1024,128]{2,1,0:T(8,128)(2,1)S(1)} %copy-done, bf16[32,1024,128]{2,1,0:T(8,128)(2,1)S(1)} %copy-done), custom_call_target="tpu_custom_call" | custom-call | flops 1073741824 | bytes 8388608 | tf_op jit(solution)/shard_map/pallas_call | solution.py:82
  38.5 0.8 collective-permute-start
  39.3 0.0 collective-permute-start.11
  39.3 0.5 collective-permute-start.12
  39.8 5.2 %collective-permute-done = bf16[16,64,128]{2,1,0:T(8,128)(2,1)} collective-permute-done((bf16[16,64,128]{2,1,0:T(8,128)(2,1)S(1)}, bf16[16,64,128]{2,1,0:T(8,128)(2,1)}, u32[]{:S(2)}, u32[]{:S(2)}) %collective-permute-start) | collective-permute-done | bytes 262176 | tf_op jit(solution)/shard_map/ppermute | solution.py:342
  45.1 1.0 %add_convert_fusion.refs_1_ = bf16[16,64,128]{2,1,0:T(8,128)(2,1)S(1)} fusion(bf16[16,64,128]{2,1,0:T(8,128)(2,1)} %collective-permute-done, bf16[16,64,128]{2,1,0:T(8,128)(2,1)S(1)} %get-tuple-element.8), kind=kLoop, calls=%fused_computation.1 | loop fusion | flops 524288 | bytes 786432 | tf_op jit(solution)/shard_map/convert_element_type | solution.py:353
  46.1 0.3 collective-permute-start.1
  46.4 0.8 iota_add_fusion
  47.2 0.0 collective-permute-done.4.refs_5_
  47.2 0.1 collective-permute-start.5
  47.3 0.0 collective-permute-done.9.refs_6_
  47.3 0.5 collective-permute-start.10
  47.8 0.1 convert_reduce_fusion
  47.9 0.1 select_reduce_fusion.refs_0_
  48.0 5.8 %collective-permute-done.1.refs_2_ = bf16[16,64,128]{2,1,0:T(8,128)(2,1)S(1)} collective-permute-done((bf16[16,64,128]{2,1,0:T(8,128)(2,1)S(1)}, bf16[16,64,128]{2,1,0:T(8,128)(2,1)S(1)}, u32[]{:S(2)}, u32[]{:S(2)}) %collective-permute-start.1) | collective-permute-done | bytes 262176 | tf_op jit(solution)/shard_map/ppermute | solution.py:342
  53.7 11.0 %shard_map.83.refs_7_ = bf16[64,64,256]{2,1,0:T(8,128)(2,1)} custom-call(s32[64]{0:T(128)S(1)} %select_reduce_fusion.refs_0_, bf16[16,64,128]{2,1,0:T(8,128)(2,1)S(1)} %add_convert_fusion.refs_1_, bf16[16,64,128]{2,1,0:T(8,128)(2,1)S(1)} %collective-permute-done.1.refs_2_, bf16[64,128]{1,0:T(8,128)(2,1)S(1)} %get-tuple-element.9.refs_3_, ...), custom_call_target="tpu_custom_call" | custom-call | flops 2013265920 | bytes 6291456 | tf_op jit(solution)/shard_map/pallas_call | solution.py:273
  64.7 0.0 collective-permute-done.11.refs_5_
  64.7 0.0 collective-permute-done.12.refs_6_
  64.7 9.6 %shard_map.84.refs_7_ = bf16[64,64,256]{2,1,0:T(8,128)(2,1)} custom-call(s32[64]{0:T(128)S(1)} %select_reduce_fusion.refs_0_, bf16[16,64,128]{2,1,0:T(8,128)(2,1)S(1)} %add_convert_fusion.refs_1_, bf16[16,64,128]{2,1,0:T(8,128)(2,1)S(1)} %collective-permute-done.1.refs_2_, ...), custom_call_target="tpu_custom_call", output_to_operand_aliasing={{}: (7, {})} | custom-call | flops 2013265920 | bytes 6291456 | tf_op jit(solution)/shard_map/pallas_call | solution.py:273
  74.3 9.6 %shard_map.85.refs_7_ = bf16[64,64,256]{2,1,0:T(8,128)(2,1)} custom-call(s32[64]{0:T(128)S(1)} %select_reduce_fusion.refs_0_, bf16[16,64,128]{2,1,0:T(8,128)(2,1)S(1)} %add_convert_fusion.refs_1_, bf16[16,64,128]{2,1,0:T(8,128)(2,1)S(1)} %collective-permute-done.1.refs_2_, ...), custom_call_target="tpu_custom_call", output_to_operand_aliasing={{}: (7, {})} | custom-call | flops 2013265920 | bytes 6291456 | tf_op jit(solution)/shard_map/pallas_call | solution.py:273
  84.0 0.0 collective-permute-done.5.refs_5_
  84.0 0.0 collective-permute-done.10.refs_6_
  84.0 7.5 %shard_map.86 = bf16[64,64,256]{2,1,0:T(8,128)(2,1)} custom-call(s32[64]{0:T(128)S(1)} %select_reduce_fusion.refs_0_, bf16[16,64,128]{2,1,0:T(8,128)(2,1)S(1)} %add_convert_fusion.refs_1_, bf16[16,64,128]{2,1,0:T(8,128)(2,1)S(1)} %collective-permute-done.1.refs_2_, bf16[64,128]{1,0:T(8,128)(2,1)S(1)} %get-tuple-element.9.refs_3_, ...), custom_call_target="tpu_custom_call", output_to_operand_aliasing={{}: (7, {})} | custom-call | flops 2013265920 | bytes 6291456 | tf_op jit(solution)/shard_map/pallas_call | solution.py:273
  (4 shorter events, 0.1 us)
Async XLA Ops:
  1.7 5.8 %collective-permute-start.2 = (bf16[1,12,64,128]{3,2,1,0:T(8,128)(2,1)S(1)}, bf16[1,12,64,128]{3,2,1,0:T(8,128)(2,1)S(1)}, u32[]{:S(2)}, u32[]{:S(2)}) collective-permute-start(bf16[1,12,64,128]{3,2,1,0:T(8,128)(2,1)S(1)} %multiply_convert_fusion), channel_id=1, source_target_pairs={{0,32},{4,12},{8,40},{12,4},{16,48},{20,28},{24,56},{28,20},{32,0}... | collective-permute-start | bytes 589832 | tf_op jit(solution)/shard_map/ppermute | solution.py:338
  3.3 8.7 %collective-permute-start.6 = (bf16[1,12,64,128]{3,2,1,0:T(8,128)(2,1)S(1)}, bf16[1,12,64,128]{3,2,1,0:T(8,128)(2,1)S(1)}, u32[]{:S(2)}, u32[]{:S(2)}) collective-permute-start(bf16[1,12,64,128]{3,2,1,0:T(8,128)(2,1)S(1)} %multiply_convert_fusion), channel_id=1, source_target_pairs={{0,96},{4,28},{8,104},{12,20},{16,112},{20,12},{24,120},{28,4},{32... | collective-permute-start | bytes 589832 | tf_op jit(solution)/shard_map/ppermute | solution.py:338
  7.5 6.9 %collective-permute-start.7 = (bf16[1,12,64,128]{3,2,1,0:T(8,128)(2,1)S(1)}, bf16[1,12,64,128]{3,2,1,0:T(8,128)(2,1)S(1)}, u32[]{:S(2)}, u32[]{:S(2)}) collective-permute-start(bf16[1,12,64,128]{3,2,1,0:T(8,128)(2,1)S(1)} %collective-permute-done.2), channel_id=1, source_target_pairs={{0,96},{4,28},{8,104},{12,20},{16,112},{20,12},{24,120},{28,4},{32... | collective-permute-start | bytes 589832 | tf_op jit(solution)/shard_map/ppermute | solution.py:338
  10.2 7.9 %collective-permute-start.3 = (bf16[2,12,64,128]{3,2,1,0:T(8,128)(2,1)S(1)}, bf16[2,12,64,128]{3,2,1,0:T(8,128)(2,1)S(1)}, u32[]{:S(2)}, u32[]{:S(2)}) collective-permute-start(bf16[2,12,64,128]{3,2,1,0:T(8,128)(2,1)S(1)} %pad_maximum_fusion.1), channel_id=1, source_target_pairs={{0,8},{4,36},{8,0},{12,44},{16,24},{20,52},{24,16},{28,60},{32,40}... | collective-permute-start | bytes 1179656 | tf_op jit(solution)/shard_map/ppermute | solution.py:338
  14.4 7.9 %collective-permute-start.8 = (bf16[2,12,64,128]{3,2,1,0:T(8,128)(2,1)S(1)}, bf16[2,12,64,128]{3,2,1,0:T(8,128)(2,1)S(1)}, u32[]{:S(2)}, u32[]{:S(2)}) collective-permute-start(bf16[2,12,64,128]{3,2,1,0:T(8,128)(2,1)S(1)} %pad_maximum_fusion.2), channel_id=1, source_target_pairs={{0,24},{4,100},{8,16},{12,108},{16,8},{20,116},{24,0},{28,124},{32... | collective-permute-start | bytes 1179656 | tf_op jit(solution)/shard_map/ppermute | solution.py:338
  18.2 29.0 %collective-permute-start.4 = (bf16[4,12,64,128]{3,2,1,0:T(8,128)(2,1)S(1)}, bf16[4,12,64,128]{3,2,1,0:T(8,128)(2,1)S(1)}, u32[]{:S(2)}, u32[]{:S(2)}) collective-permute-start(bf16[4,12,64,128]{3,2,1,0:T(8,128)(2,1)S(1)} %pad_maximum_fusion.refs_5_), channel_id=1, source_target_pairs={{0,24},{4,100},{8,16},{12,108},{16,8},{20,116},{24,0},{28,124},{32... | collective-permute-start | bytes 2359304 | tf_op jit(solution)/shard_map/ppermute | solution.py:338
  22.3 25.0 %collective-permute-start.9 = (bf16[4,12,64,128]{3,2,1,0:T(8,128)(2,1)S(1)}, bf16[4,12,64,128]{3,2,1,0:T(8,128)(2,1)S(1)}, u32[]{:S(2)}, u32[]{:S(2)}) collective-permute-start(bf16[4,12,64,128]{3,2,1,0:T(8,128)(2,1)S(1)} %constant_dynamic-update-slice_fusion.refs_6_), channel_id=1, source_target_pairs={{0,8},{4,36},{8,0},{12,44},{16,24},{20,52},{24,16},{28,60},{32,40}... | collective-permute-start | bytes 2359304 | tf_op jit(solution)/shard_map/ppermute | solution.py:338
  25.2 3.4 %copy-start = (bf16[32,1024,128]{2,1,0:T(8,128)(2,1)S(1)}, bf16[32,1024,128]{2,1,0:T(8,128)(2,1)}, u32[]{:S(2)}) copy-start(bf16[32,1024,128]{2,1,0:T(8,128)(2,1)} %constant.13.clone.first.second) | copy-start | bytes 25165828
  28.6 3.4 %copy-start.1 = (bf16[16,256,1024]{2,1,0:T(8,128)(2,1)S(1)}, bf16[16,256,1024]{2,1,0:T(8,128)(2,1)}, u32[]{:S(2)}) copy-start(bf16[16,256,1024]{2,1,0:T(8,128)(2,1)} %masks.1) | copy-start | bytes 25165828
  38.5 6.6 %collective-permute-start = (bf16[16,64,128]{2,1,0:T(8,128)(2,1)S(1)}, bf16[16,64,128]{2,1,0:T(8,128)(2,1)}, u32[]{:S(2)}, u32[]{:S(2)}) collective-permute-start(bf16[16,64,128]{2,1,0:T(8,128)(2,1)S(1)} %get-tuple-element.8), channel_id=1, source_target_pairs={{0,1},{1,0},{2,3},{3,2},{4,5},{5,4},{6,7},{7,6},{8,9},{9,8},{10,11... | collective-permute-start | bytes 786440 | tf_op jit(solution)/shard_map/ppermute | solution.py:342
  39.3 25.4 %collective-permute-start.11 = (bf16[4,12,64,128]{3,2,1,0:T(8,128)(2,1)S(1)}, bf16[4,12,64,128]{3,2,1,0:T(8,128)(2,1)S(1)}, u32[]{:S(2)}, u32[]{:S(2)}) collective-permute-start(bf16[4,12,64,128]{3,2,1,0:T(8,128)(2,1)S(1)} %pad_maximum_fusion.refs_5_), channel_id=1, source_target_pairs={{0,4},{4,0},{8,12},{12,8},{16,20},{20,16},{24,28},{28,24},{32,36},... | collective-permute-start | bytes 2359304 | tf_op jit(solution)/shard_map/ppermute | solution.py:339
  39.3 25.4 %collective-permute-start.12 = (bf16[4,12,64,128]{3,2,1,0:T(8,128)(2,1)S(1)}, bf16[4,12,64,128]{3,2,1,0:T(8,128)(2,1)S(1)}, u32[]{:S(2)}, u32[]{:S(2)}) collective-permute-start(bf16[4,12,64,128]{3,2,1,0:T(8,128)(2,1)S(1)} %constant_dynamic-update-slice_fusion.refs_6_), channel_id=1, source_target_pairs={{0,4},{4,0},{8,12},{12,8},{16,20},{20,16},{24,28},{28,24},{32,36},... | collective-permute-start | bytes 2359304 | tf_op jit(solution)/shard_map/ppermute | solution.py:339
  46.1 7.7 %collective-permute-start.1 = (bf16[16,64,128]{2,1,0:T(8,128)(2,1)S(1)}, bf16[16,64,128]{2,1,0:T(8,128)(2,1)S(1)}, u32[]{:S(2)}, u32[]{:S(2)}) collective-permute-start(bf16[16,64,128]{2,1,0:T(8,128)(2,1)S(1)} %add_convert_fusion.refs_1_), channel_id=1, source_target_pairs={{0,3},{1,2},{2,1},{3,0},{4,7},{5,6},{6,5},{7,4},{8,11},{9,10},{10,... | collective-permute-start | bytes 786440 | tf_op jit(solution)/shard_map/ppermute | solution.py:342
  47.2 36.8 %collective-permute-start.5 = (bf16[4,12,64,128]{3,2,1,0:T(8,128)(2,1)S(1)}, bf16[4,12,64,128]{3,2,1,0:T(8,128)(2,1)S(1)}, u32[]{:S(2)}, u32[]{:S(2)}) collective-permute-start(bf16[4,12,64,128]{3,2,1,0:T(8,128)(2,1)S(1)} %collective-permute-done.4.refs_5_), channel_id=1, source_target_pairs={{0,4},{4,0},{8,12},{12,8},{16,20},{20,16},{24,28},{28,24},{32,36},... | collective-permute-start | bytes 2359304 | tf_op jit(solution)/shard_map/ppermute | solution.py:339
  47.3 36.7 %collective-permute-start.10 = (bf16[4,12,64,128]{3,2,1,0:T(8,128)(2,1)S(1)}, bf16[4,12,64,128]{3,2,1,0:T(8,128)(2,1)S(1)}, u32[]{:S(2)}, u32[]{:S(2)}) collective-permute-start(bf16[4,12,64,128]{3,2,1,0:T(8,128)(2,1)S(1)} %collective-permute-done.9.refs_6_), channel_id=1, source_target_pairs={{0,4},{4,0},{8,12},{12,8},{16,20},{20,16},{24,28},{28,24},{32,36},... | collective-permute-start | bytes 2359304 | tf_op jit(solution)/shard_map/ppermute | solution.py:339
